TPU v7x, 32 devices: a whole 2x2x4 slice. The times are simulated.
32 devices in a mesh: groups: 2 (over y), st: 4 (over z), br: 2 (over x), pol: 2 (over core).
Axes of the slice: x: 2, y: 2, z: 4, core: 2. Of those that a mesh axis runs over, the one named last changes fastest.
Arguments:
- samples: bfloat16 [2, 1024, 32768], P(None, ('groups', 'st', 'pol'), 'br'), parts along dimension 1, may hold values from -6 to 6
- tap_table: int32 [12, 128], replicated, may hold values from -4096 to 4096
- station_flags: int32 [512], P(('st', 'pol')), may hold values 0 or 1
- beam_delays: int32 [512, 512], replicated, may hold values from 0 to 4095
Outputs:
- visibilities: float32 [1024, 128, 2, 512], P(('groups', 'br'), ('st', 'pol')), parts along dimension 0
- beam_series: float32 [1024, 256, 256], P(('groups', 'st', 'pol'), 'br'), parts along dimension 0
There are 2 independent parts, one for each index of `groups`. A program takes and returns all parts, laid end to end along the dimension named above; an argument that names none is the same for every part. Nothing has to cross between parts.
All inputs are finite; a program needn't handle non-finite values. No bound on the sum of `station_flags` on one device may be relied on, other than what follows from the above.
Results may differ from a plain program's by a relative error of at most 0.012.
Values may be sent and summed in bfloat16 or wider, within the bound.
A program may use at most 128 MiB of HBM per device.

v0:
```python
import math

import jax
import jax.numpy as jnp
from jax import lax
from jax.sharding import PartitionSpec as P

NSP = 512
NCH = 128
NTAP = 12


tap_scale = 4096.0


def shifted(block, axis, distance):
    devices = range(lax.axis_size(axis))
    route = [(i - distance, i) for i in devices if i - distance in devices]
    return lax.ppermute(block, axis, route)


def forward_table(nchan, per_owner):
    out_index = jnp.arange(2 * nchan)
    owner_block = out_index // (2 * per_owner)
    half_index = out_index // per_owner % 2
    channel = owner_block * per_owner + out_index % per_owner
    freq_index = jnp.arange(nchan)
    phase_index = freq_index[:, None] * channel[None, :] % nchan
    phase_angle = 2.0 * math.pi * phase_index.astype(jnp.float32) / nchan
    norm = 1.0 / math.sqrt(nchan)
    cos_part = jnp.cos(phase_angle) * norm
    sin_part = jnp.sin(phase_angle) * norm
    real_in = jnp.where(half_index[None, :] == 0, cos_part, -sin_part)
    imag_in = jnp.where(half_index[None, :] == 0, sin_part, cos_part)
    return jnp.stack([real_in, imag_in])


def inverse_table(nchan):
    out_index = jnp.arange(2 * nchan)
    sample = out_index % nchan
    half_index = out_index // nchan
    channel = jnp.arange(nchan)
    phase_index = channel[:, None] * sample[None, :] % nchan
    phase_angle = 2.0 * math.pi * phase_index.astype(jnp.float32) / nchan
    norm = 1.0 / math.sqrt(nchan)
    cos_part = jnp.cos(phase_angle) * norm
    sin_part = jnp.sin(phase_angle) * norm
    real_in = jnp.where(half_index[None, :] == 0, cos_part, sin_part)
    imag_in = jnp.where(half_index[None, :] == 0, -sin_part, cos_part)
    return jnp.stack([real_in, imag_in]).astype(jnp.bfloat16)


def beam_weights(beam_delays, channel_ids, ninputs, nchan):
    phase_index = beam_delays[None, :, :] * channel_ids[:, None, None] % nchan
    phase_angle = 2.0 * math.pi * phase_index.astype(jnp.float32) / nchan
    norm = 1.0 / math.sqrt(ninputs)
    weight_re = jnp.cos(phase_angle) * norm
    weight_im = -jnp.sin(phase_angle) * norm
    first_row = jnp.stack([weight_re, -weight_im], axis=1)
    second_row = jnp.stack([weight_im, weight_re], axis=1)
    return jnp.stack([first_row, second_row], axis=1).astype(jnp.bfloat16)


def local(samples, tap_table, station_flags, beam_delays):
    inputs_here = samples.shape[1]
    sample_count = samples.shape[2]
    spectra_dev = sample_count // NCH
    owners_st = lax.axis_size("st")
    owners_pol = lax.axis_size("pol")
    owners = owners_st * owners_pol
    per_owner = NCH // owners
    tail_len = (NTAP - 1) * NCH
    tail = samples[:, :, sample_count - tail_len :]
    before = shifted(tail, "br", 1)
    extended = jnp.concatenate([before, samples], axis=2).astype(jnp.float32)
    extended = extended.reshape(2, inputs_here, spectra_dev + NTAP - 1, NCH)
    coefficients = tap_table.astype(jnp.float32) / tap_scale
    filtered = jnp.zeros((2, inputs_here, spectra_dev, NCH), jnp.float32)
    for tap_index in range(NTAP):
        begin = NTAP - 1 - tap_index
        filtered = (
            filtered
            + coefficients[tap_index][None, None, None, :]
            * extended[:, :, begin : begin + spectra_dev, :]
        )
    table = forward_table(NCH, per_owner)
    spectra = jnp.einsum("rstk,rko->ost", filtered, table, precision=lax.Precision.HIGHEST)
    spectra = (spectra * station_flags.astype(jnp.float32)[None, :, None]).astype(jnp.bfloat16)
    outgoing = spectra.reshape(owners, 2, per_owner, inputs_here, spectra_dev)
    arrived = lax.all_to_all(outgoing, ("st", "pol"), split_axis=0, concat_axis=3, tiled=True)
    turned = arrived.reshape(2, per_owner, NSP, spectra_dev)
    time_scale = 1.0 / (spectra_dev * lax.axis_size("br"))
    right_side = jnp.concatenate([turned[0], turned[1]], axis=2)
    left_imag_all = jnp.concatenate([turned[1], -turned[0]], axis=2)
    vis_real = jnp.einsum(
        "cik,cjk->icj", right_side, right_side, preferred_element_type=jnp.float32
    )
    vis_imag = jnp.einsum(
        "cik,cjk->icj", left_imag_all, right_side, preferred_element_type=jnp.float32
    )
    visibilities = lax.psum_scatter(
        (jnp.stack([vis_real, vis_imag], axis=2) * time_scale).astype(jnp.bfloat16),
        "br",
        scatter_dimension=0,
        tiled=True,
    ).astype(jnp.float32)
    channel_ids = lax.axis_index(("st", "pol")) * per_owner + jnp.arange(per_owner, dtype=jnp.int32)
    weights = beam_weights(beam_delays, channel_ids, NSP, NCH)
    beam_volt = jnp.einsum(
        "corbi,rcit->boct", weights, turned, preferred_element_type=jnp.float32
    ).astype(jnp.bfloat16)
    synth_table = inverse_table(NCH)
    beam_series = jnp.einsum(
        "brck,rco->bko",
        lax.all_to_all(beam_volt, ("st", "pol"), split_axis=0, concat_axis=2, tiled=True),
        synth_table,
        preferred_element_type=jnp.float32,
    )
    return (visibilities, beam_series)


def solution(mesh):
    return jax.shard_map(
        local,
        mesh=mesh,
        in_specs=(P(None, ("groups", "st", "pol"), "br"), P(), P(("st", "pol")), P()),
        out_specs=(
            P(("groups", "br"), ("st", "pol"), None, None),
            P(("groups", "st", "pol"), "br", None),
        ),
        check_vma=False,
    )
```

profile of v0, /device:TPU:0, one launch (start us, length us, event | category | flops | bytes accessed | tf_op | source)
XLA Modules:
  0.0 466.4 jit_solution(16813596114835795058)
XLA Ops:
  7.2 0.0 reduce-scatter.2.cloned.1.call-start
  7.2 1.0 slice.86
  8.2 4.9 %collective-permute-start = (bf16[2,64,1408]{2,1,0:T(8,128)(2,1)S(1)}, bf16[2,64,1408]{2,1,0:T(8,128)(2,1)S(1)}, u32[]{:S(2)}, u32[]{:S(2)}) collective-permute-start(bf16[2,64,1408]{2,1,0:T(8,128)(2,1)S(1)} %slice.86), channel_id=1, source_target_pairs={{0,2},{1,3},{4,6},{5,7},{8,10},{9,11},{12,14},{13,15},{16,18},{17,... | collective-permute-start | bytes 1081352 | tf_op jit(solution)/shard_map/ppermute | solution.py:19
  13.1 0.7 convert_multiply_fusion
  13.8 0.7 convert_element_type.84
  14.5 0.6 negate_select_fusion.5
  15.1 5.6 %collective-permute-done = bf16[2,64,1408]{2,1,0:T(8,128)(2,1)S(1)} collective-permute-done((bf16[2,64,1408]{2,1,0:T(8,128)(2,1)S(1)}, bf16[2,64,1408]{2,1,0:T(8,128)(2,1)S(1)}, u32[]{:S(2)}, u32[]{:S(2)}) %collective-permute-start) | collective-permute-done | bytes 360480 | tf_op jit(solution)/shard_map/ppermute | solution.py:19
  20.7 6.3 %maximum_convert_fusion = f32[2,64,17792]{2,1,0:T(8,128)} fusion(bf16[2,64,16384]{2,1,0:T(8,128)(2,1)} %param.4, bf16[2,64,1408]{2,1,0:T(8,128)(2,1)S(1)} %collective-permute-done), kind=kLoop, calls=%fused_computation.49 | loop fusion | flops 9109504 | bytes 13664256 | tf_op jit(solution)/shard_map/convert_element_type | solution.py:75
  27.0 9.7 %reshape.480 = f32[2,64,139,128]{3,2,1,0:T(8,128)} reshape(f32[2,64,17792]{2,1,0:T(8,128)} %maximum_convert_fusion) | data formatting | bytes 18219008 | tf_op jit(solution)/shard_map/convert_element_type | solution.py:75
  36.8 40.6 %fusion.32 = bf16[256,64,128]{2,0,1:T(8,128)(2,1)} fusion(f32[64]{0:T(128)S(1)} %convert_element_type.84, f32[2,64,139,128]{3,2,1,0:T(8,128)} %reshape.480, f32[128]{0:T(128)S(1)} %get-tuple-element.18, f32[128]{0:T(128)S(1)} %get-tuple-element.19, f32[128]{0:T(128)S(1)} %get-tuple-element.20, f32[128]{0:T(128)S(1)} %get-tuple-element.21, ...), kind=kOutput, calls=%fused_computation.47 | convolution fusion | flops 6494945280 | bytes 105126144 | tf_op jit(solution)/shard_map/rstk,rko->ost/dot_general | solution.py:87
  77.4 4.9 %copy.35 = bf16[8,2,16,64,128]{4,3,2,1,0:T(8,128)(2,1)S(1)} copy(bf16[8,2,16,64,128]{4,2,1,0,3:T(8,128)(2,1)} %bitcast.88) | data formatting | bytes 8388608 | tf_op jit(solution)/shard_map/reshape | solution.py:89
  82.3 98.7 %all_to_all.33 = bf16[8,2,16,64,128]{4,3,2,1,0:T(8,128)(2,1)S(1)} all-to-all(bf16[8,2,16,64,128]{4,3,2,1,0:T(8,128)(2,1)S(1)} %copy.35), channel_id=1, replica_groups=mesh['groups'=2,'st'=4,'br'=2,'pol'=2] {'st','pol'}, dimensions={0} | all-to-all | bytes 8388608 | tf_op jit(solution)/shard_map/all_to_all | solution.py:90
  181.0 1.4 copy.60
  182.4 0.0 copy-start
  182.4 2.0 copy-done
  184.4 1.0 fusion.90
  185.4 0.6 neg.48
  186.0 7.0 %convolution_bitcast_fusion.1 = f32[512,16,1,512]{0,3,1,2:T(8,128)} fusion(bf16[16,512,128]{2,1,0:T(8,128)(2,1)S(1)} %bitcast.82, bf16[16,512,128]{2,1,0:T(8,128)(2,1)S(1)} %bitcast.80), kind=kOutput, calls=%fused_computation.21 | convolution fusion | flops 2155872256 | bytes 20971520 | tf_op jit(solution)/shard_map/cik,cjk->icj/dot_general | solution.py:95
  193.0 7.4 %convolution_bitcast_fusion = f32[512,16,1,512]{0,3,1,2:T(8,128)} fusion(bf16[16,512,128]{2,1,0:T(8,128)(2,1)S(1)} %neg.48, bf16[16,512,128]{2,1,0:T(8,128)(2,1)S(1)} %bitcast.83, bf16[16,512,128]{2,1,0:T(8,128)(2,1)S(1)} %bitcast.81), kind=kOutput, calls=%fused_computation.20 | convolution fusion | flops 2164260864 | bytes 23068672 | tf_op jit(solution)/shard_map/cik,cjk->icj/dot_general | solution.py:98
  200.4 18.6 %fusion = bf16[512,16,2,512]{0,3,1,2:T(8,128)(2,1)} fusion(f32[512,16,1,512]{0,3,1,2:T(8,128)} %convolution_bitcast_fusion, f32[512,16,1,512]{0,3,1,2:T(8,128)} %convolution_bitcast_fusion.1), kind=kLoop, calls=%fused_computation.1 | loop fusion | flops 25165824 | bytes 50331648 | tf_op jit(solution)/shard_map/convert_element_type | solution.py:102
  219.1 0.0 copy-start.1
  219.1 0.0 reduce-scatter.2.cloned.1.call-update
  219.1 1.2 copy-done.1
  220.3 68.6 %negate_convert_fusion = (bf16[16,1,512,512]{3,2,1,0:T(8,128)(2,1)S(1)}, bf16[16,1,512,512]{3,2,1,0:T(8,128)(2,1)S(1)}, bf16[16,1,512,512]{3,2,1,0:T(8,128)(2,1)S(1)}) fusion(s32[16]{0:T(128)S(1)} %iota_add_fusion, s32[512,512]{1,0:T(8,128)S(1)} %copy-done.1), kind=kLoop, calls=%fused_computation.16 | loop fusion | flops 88080384 | bytes 26214464 | tf_op jit(solution)/shard_map/convert.10
  288.9 11.3 %maximum_bitcast_fusion = (bf16[16,1,2,512,512]{4,3,2,1,0:T(8,128)(2,1)}, bf16[16,1,2,512,512]{4,3,2,1,0:T(8,128)(2,1)}) fusion(bf16[16,1,512,512]{3,2,1,0:T(8,128)(2,1)S(1)} %get-tuple-element.14, bf16[16,1,512,512]{3,2,1,0:T(8,128)(2,1)S(1)} %get-tuple-element.16, bf16[16,1,512,512]{3,2,1,0:T(8,128)(2,1)S(1)} %get-tuple-element.15), kind=kLoop, calls=%fused_computation.14 | loop fusion | flops 16777216 | bytes 58720256 | tf_op jit(solution)/shard_map/stack | solution.py:61
  300.2 19.0 %fusion.33 = bf16[512,2,16,128]{0,3,1,2:T(8,128)(2,1)} fusion(bf16[16,1,2,512,512]{4,3,2,1,0:T(8,128)(2,1)} %get-tuple-element.9, bf16[16,1,2,512,512]{4,3,2,1,0:T(8,128)(2,1)} %get-tuple-element.8, bf16[2,16,512,128,1]{3,2,1,0,4:T(8,128)(2,1)} %bitcast.86), kind=kOutput, calls=%fused_computation.50 | convolution fusion | flops 4364173312 | bytes 41943040 | tf_op jit(solution)/shard_map/corbi,rcit->boct/dot_general | solution.py:109
  319.1 11.2 %copy.39 = bf16[512,2,16,128]{3,1,2,0:T(2,128)(2,1)} copy(bf16[512,2,16,128]{0,3,1,2:T(8,128)(2,1)} %fusion.33) | data formatting | bytes 8388608 | tf_op jit(solution)/shard_map/convert_element_type | solution.py:111
  330.3 4.8 %all-to-all-start.1 = ((bf16[512,2,16,128]{3,1,2,0:T(2,128)(2,1)}), bf16[512,2,16,128]{3,1,2,0:T(2,128)(2,1)}, u32[]{:S(2)}, u32[]{:S(2)}) async-start(bf16[512,2,16,128]{3,1,2,0:T(2,128)(2,1)} %copy.39), calls=%async_computation.2 | async-start | bytes 8388608 | tf_op jit(solution)/shard_map/all_to_all | solution.py:115
  335.1 0.6 select_convert_fusion.1
  335.8 93.1 %all-to-all-done.1 = bf16[512,2,16,128]{3,1,2,0:T(2,128)(2,1)} async-done(((bf16[512,2,16,128]{3,1,2,0:T(2,128)(2,1)}), bf16[512,2,16,128]{3,1,2,0:T(2,128)(2,1)}, u32[]{:S(2)}, u32[]{:S(2)}) %all-to-all-start.1) | async-done | bytes 4194336 | tf_op jit(solution)/shard_map/all_to_all | solution.py:115
  428.9 2.7 copy.40
  431.6 1.2 copy.41
  432.9 4.7 %convolution_bitcast_fusion.2 = f32[64,128,256]{2,1,0:T(8,128)} fusion(bf16[64,2,128,128]{3,2,1,0:T(8,128)(2,1)S(1)} %bitcast.84, bf16[1,128,256]{1,2,0:T(8,128)(2,1)S(1)} %get-tuple-element.30, bf16[1,128,256]{1,2,0:T(8,128)(2,1)S(1)} %get-tuple-element.29), kind=kOutput, calls=%fused_computation.68 | convolution fusion | flops 1073807360 | bytes 12713984 | tf_op jit(solution)/shard_map/brck,rco->bko/dot_general | solution.py:113
  437.6 0.0 reduce-scatter.2.cloned.1.call-done
  437.6 22.0 %copy.44 = f32[256,16,2,512]{3,2,1,0:T(2,128)} copy(bf16[256,16,2,512]{0,3,1,2:T(8,128)(2,1)} %reduce-scatter.2.cloned.1.call-done) | data formatting | bytes 25165824
  (6 shorter events, 0.0 us)
Async XLA Ops:
  7.2 430.4 %reduce-scatter.2.cloned.1.call-start = ((), (), s32[]{:S(2)}) async-start(), calls=%async_computation.3 | async-start | bytes 25165824 | tf_op jit(solution)/shard_map/reduce_scatter | solution.py:101
  8.2 12.5 %collective-permute-start = (bf16[2,64,1408]{2,1,0:T(8,128)(2,1)S(1)}, bf16[2,64,1408]{2,1,0:T(8,128)(2,1)S(1)}, u32[]{:S(2)}, u32[]{:S(2)}) collective-permute-start(bf16[2,64,1408]{2,1,0:T(8,128)(2,1)S(1)} %slice.86), channel_id=1, source_target_pairs={{0,2},{1,3},{4,6},{5,7},{8,10},{9,11},{12,14},{13,15},{16,18},{17,... | collective-permute-start | bytes 1081352 | tf_op jit(solution)/shard_map/ppermute | solution.py:19
  182.4 2.0 copy-start
  219.1 1.2 copy-start.1
  330.3 98.6 %all-to-all-start.1 = ((bf16[512,2,16,128]{3,1,2,0:T(2,128)(2,1)}), bf16[512,2,16,128]{3,1,2,0:T(2,128)(2,1)}, u32[]{:S(2)}, u32[]{:S(2)}) async-start(bf16[512,2,16,128]{3,1,2,0:T(2,128)(2,1)} %copy.39), calls=%async_computation.2 | async-start | bytes 8388608 | tf_op jit(solution)/shard_map/all_to_all | solution.py:115
Sparse Core Ops, SparseCore 0:
  219.2 188.9 reduce-scatter.1
where the time goes:
time: 468 us; the launch traced here: 466 us
  other arithmetic  108 us (23%)
  waiting for transfers between devices  98.8 us (21%)
  blocking collectives  98.7 us (21%)
  matrix products  78.8 us (17%)
  local copies, waits for them, and re-layouts  58.3 us (12%)
  between operations  14.1 us (3%)
  starting transfers between devices  9.68 us (2%)
    all_to_all x1, blocking collectives, local(): lax.all_to_all(outgoing, ('st', 'pol'), split_axis=0, concat_axis=3, tile...  98.7 us
    all_to_all x1, waiting for transfers between devices, local(): lax.all_to_all(beam_volt, ('st', 'pol'), split_axis=0, concat_axis=2, til...  93.1 us
    another operation x2, other arithmetic  69.2 us
    dot_general x1, matrix products, local(): jnp.einsum('rstk,rko->ost', filtered, table, precision=lax.Precision.HIGH...  40.6 us
    unnamed x5, local copies, waits for them, and re-layouts  25.1 us
    dot_general x1, matrix products, local(): jnp.einsum('corbi,rcit->boct', weights, turned, preferred_element_type=jn...  19 us
    convert_element_type x1, other arithmetic, local(): (jnp.stack([vis_real, vis_imag], axis=2) * time_scale).astype(jnp.bfloat16)  18.6 us
    another operation x1, other arithmetic, beam_weights(): return jnp.stack([first_row, second_row], axis=1).astype(jnp.bfloat16)  11.3 us
  transfers between devices with their start and end apart: 3, of which 2 were waited for; matrix products, arithmetic and copies ran while one was open for 26% of the time, Pallas kernels for 0%

commit v1 on v0

v1 whole, which is shorter than its diff:
```python
import functools
import math

import jax
import jax.numpy as jnp
from jax import lax
from jax.experimental import pallas as pl
from jax.experimental.pallas import tpu as pltpu
from jax.sharding import PartitionSpec as P

tap_scale = 4096.0
LANES = 128
GROUP = 16
VMEM = pltpu.VMEM


def forward_table(nchan, per_owner):
    out_index = jnp.arange(2 * nchan)
    owner_block = out_index // (2 * per_owner)
    half_index = out_index // per_owner % 2
    channel = owner_block * per_owner + out_index % per_owner
    freq_index = jnp.arange(nchan)
    phase_index = channel[:, None] * freq_index[None, :] % nchan
    phase_angle = 2.0 * math.pi * phase_index.astype(jnp.float32) / nchan
    norm = 1.0 / math.sqrt(nchan)
    cos_part = jnp.cos(phase_angle) * norm
    sin_part = jnp.sin(phase_angle) * norm
    real_in = jnp.where(half_index[:, None] == 0, cos_part, -sin_part)
    imag_in = jnp.where(half_index[:, None] == 0, sin_part, cos_part)
    return jnp.concatenate([real_in, imag_in], axis=1)


def inverse_table(nchan):
    out_index = jnp.arange(2 * nchan)
    sample = out_index % nchan
    half_index = out_index // nchan
    channel = jnp.arange(nchan)
    phase_index = channel[:, None] * sample[None, :] % nchan
    phase_angle = 2.0 * math.pi * phase_index.astype(jnp.float32) / nchan
    norm = 1.0 / math.sqrt(nchan)
    cos_part = jnp.cos(phase_angle) * norm
    sin_part = jnp.sin(phase_angle) * norm
    real_in = jnp.where(half_index[None, :] == 0, cos_part, sin_part)
    imag_in = jnp.where(half_index[None, :] == 0, -sin_part, cos_part)
    return jnp.stack([real_in, imag_in]).astype(jnp.bfloat16)


def filter_group(ntap, g, samples, before, coef, flags, table_hi, table_lo, ext, filt, turn):
    nspec = samples.shape[2] // LANES
    hist = ntap - 1
    rows = pl.ds(pl.multiple_of(g * GROUP, GROUP), GROUP)
    block = 8
    for r in range(2):
        for t in range(hist):
            ext[t] = before[r, rows, t * LANES : (t + 1) * LANES].astype(jnp.float32)

        @pl.loop(0, nspec // block)
        def _(tb):
            for u in range(block):
                t = tb * block + u
                lanes = pl.ds(pl.multiple_of(t * LANES, LANES), LANES)
                ext[hist + t] = samples[r, rows, lanes].astype(jnp.float32)

        for h in range(GROUP // 8):
            used = flags[pl.ds(pl.multiple_of(g * GROUP + h * 8, 8), 8), :]

            @pl.loop(0, nspec // block)
            def _(tb):
                t0 = tb * block
                window = [ext[t0 + u, h * 8 : h * 8 + 8, :] for u in range(block + hist)]
                for u in range(block):
                    total = coef[0:1, :] * window[hist + u]
                    for j in range(1, ntap):
                        total = total + coef[j : j + 1, :] * window[hist + u - j]
                    filt[r, pl.ds(h * 8 * nspec + t0 + u, 8, stride=nspec), :] = total * used

    @pl.loop(0, GROUP)
    def _(s):
        at = pl.ds(pl.multiple_of(s * nspec, nspec), nspec)
        values = jnp.concatenate([filt[0, at, :], filt[1, at, :]], axis=1)
        high = values.astype(jnp.bfloat16)
        low = (values - high.astype(jnp.float32)).astype(jnp.bfloat16)

        def product(a, b):
            return lax.dot_general(a, b, (((1,), (1,)), ((), ())), preferred_element_type=jnp.float32)

        out = product(table_lo[...], high) + product(table_hi[...], low) + product(table_hi[...], high)
        turn[pl.ds(s, out.shape[0], stride=GROUP), :] = out


def filter_kernel(ntap, samples, before, coef, flags, table_hi, table_lo, out, ext, filt, turn):
    nrow = out.shape[0]

    @pl.loop(0, samples.shape[1] // GROUP)
    def _(g):
        filter_group(ntap, g, samples, before, coef, flags, table_hi, table_lo, ext, filt, turn)
        rows = pl.ds(pl.multiple_of(g * GROUP, GROUP), GROUP)

        @pl.loop(0, nrow // 16)
        def _(o):
            part = turn[pl.ds(pl.multiple_of(o * 16 * GROUP, 16 * GROUP), 16 * GROUP), :]
            out[pl.ds(o * 16, 16), rows, :] = part.reshape(16, GROUP, LANES).astype(jnp.bfloat16)


def cosine(phase, nchan):
    z = (jnp.abs(phase - nchan // 2) - nchan // 4).astype(jnp.float32) * (2.0 * math.pi / nchan)
    z2 = z * z
    total = jnp.full_like(z, -1.0 / math.factorial(11))
    for n in (9, 7, 5, 3, 1):
        total = total * z2 + (-1.0) ** ((n - 1) // 2) / math.factorial(n)
    return total * z


def beam_kernel(nchan, delays, x, out, w_re, w_im, s_re, s_im):
    c = pl.program_id(0)
    per_owner = pl.num_programs(0)
    nbeam, nin = delays.shape
    mask = nchan - 1

    @pl.when(c == 0)
    def _():
        owner = lax.axis_index("st") * lax.axis_size("pol") + lax.axis_index("pol")
        d = delays[...]
        norm = 1.0 / math.sqrt(nin)
        step = d & mask
        s_re[...] = cosine(step, nchan)
        s_im[...] = -cosine((step - nchan // 4) & mask, nchan)
        first = (d * (owner * per_owner)) & mask
        w_re[...] = cosine(first, nchan) * norm
        w_im[...] = -cosine((first - nchan // 4) & mask, nchan) * norm

    re, im = w_re[...], w_im[...]
    left = jnp.concatenate([re.astype(jnp.bfloat16), (-im).astype(jnp.bfloat16)], axis=1)
    x_re, x_im = x[0, 0], x[1, 0]
    right = jnp.concatenate(
        [jnp.concatenate([x_re, x_im], axis=1), jnp.concatenate([x_im, -x_re], axis=1)], axis=0
    )
    volt = jnp.dot(left, right, preferred_element_type=jnp.float32).astype(jnp.bfloat16)
    nspec = x_re.shape[1]
    owners, per_beam = out.shape[0], out.shape[3]
    for o in range(owners):
        for r in range(2):
            out[o, 0, r] = volt[o * per_beam : (o + 1) * per_beam, r * nspec : (r + 1) * nspec]
    a, b = s_re[...], s_im[...]
    w_re[...] = re * a - im * b
    w_im[...] = re * b + im * a


def beams(beam_delays, turned, owners, nchan):
    _, per_owner, nin, nspec = turned.shape
    nbeam = beam_delays.shape[0]
    plane = pltpu.VMEM((nbeam, nin), jnp.float32)
    return pl.pallas_call(
        functools.partial(beam_kernel, nchan),
        grid=(per_owner,),
        out_shape=jax.ShapeDtypeStruct((owners, per_owner, 2, nbeam // owners, nspec), jnp.bfloat16),
        in_specs=[
            pl.BlockSpec((nbeam, nin), lambda c: (0, 0)),
            pl.BlockSpec((2, 1, nin, nspec), lambda c: (0, c, 0, 0)),
        ],
        out_specs=pl.BlockSpec((owners, 1, 2, nbeam // owners, nspec), lambda c: (0, c, 0, 0, 0)),
        scratch_shapes=[plane] * 4,
        compiler_params=pltpu.CompilerParams(vmem_limit_bytes=40 * 2**20),
        cost_estimate=pl.CostEstimate(flops=2**32, bytes_accessed=2**23, transcendentals=0),
    )(beam_delays, turned)


def local(samples, tap_table, station_flags, beam_delays):
    inputs_here = samples.shape[1]
    sample_count = samples.shape[2]
    ntap, nchan = tap_table.shape
    nin = beam_delays.shape[1]
    spectra_dev = sample_count // nchan
    owners = lax.axis_size("st") * lax.axis_size("pol")
    blocks = lax.axis_size("br")
    per_owner = nchan // owners
    tail_len = (ntap - 1) * nchan
    tail = samples[:, :, sample_count - tail_len :]
    before = lax.ppermute(tail, "br", [(i, i + 1) for i in range(blocks - 1)])
    coefficients = tap_table.astype(jnp.float32) / tap_scale
    flags = jnp.broadcast_to(station_flags.astype(jnp.float32)[:, None], (inputs_here, LANES))
    table = forward_table(nchan, per_owner)
    table_hi = table.astype(jnp.bfloat16)
    table_lo = (table - table_hi.astype(jnp.float32)).astype(jnp.bfloat16)
    spectra = pl.pallas_call(
        functools.partial(filter_kernel, ntap),
        out_shape=jax.ShapeDtypeStruct((2 * nchan, inputs_here, spectra_dev), jnp.bfloat16),
        scratch_shapes=[
            pltpu.VMEM((spectra_dev + ntap - 1, GROUP, LANES), jnp.float32),
            pltpu.VMEM((2, GROUP * spectra_dev, LANES), jnp.float32),
            pltpu.VMEM((2 * nchan * GROUP, LANES), jnp.float32),
        ],
        in_specs=[pl.BlockSpec(memory_space=VMEM)] * 6,
        out_specs=pl.BlockSpec(memory_space=VMEM),
        compiler_params=pltpu.CompilerParams(vmem_limit_bytes=40 * 2**20),
    )(samples, before, coefficients, flags, table_hi, table_lo)
    outgoing = spectra.reshape(owners, 2, per_owner, inputs_here, spectra_dev)
    arrived = lax.all_to_all(outgoing, ("st", "pol"), split_axis=0, concat_axis=3, tiled=True)
    turned = arrived.reshape(2, per_owner, nin, spectra_dev)

    volts = beams(beam_delays, turned, owners, nchan)
    series_in = lax.all_to_all(volts, ("st", "pol"), split_axis=0, concat_axis=0, tiled=True)

    parts = [turned]
    for k in range(1, blocks):
        parts.append(lax.ppermute(turned, "br", [(i, (i + k) % blocks) for i in range(blocks)]))
    right = jnp.concatenate([p[r] for p in parts for r in (0, 1)], axis=2)
    left_imag = jnp.concatenate([q for p in parts for q in (p[1], -p[0])], axis=2)
    rows_here = nin // blocks
    first_row = lax.axis_index("br") * rows_here
    left = lax.dynamic_slice_in_dim(right, first_row, rows_here, 1)
    left_imag = lax.dynamic_slice_in_dim(left_imag, first_row, rows_here, 1)
    time_scale = 1.0 / (spectra_dev * blocks)
    vis_real = jnp.einsum("cik,cjk->icj", left, right, preferred_element_type=jnp.float32)
    vis_imag = jnp.einsum("cik,cjk->icj", left_imag, right, preferred_element_type=jnp.float32)
    visibilities = jnp.stack([vis_real, vis_imag], axis=2) * time_scale

    series_in = series_in.reshape(nchan, 2, -1, spectra_dev)
    beam_series = jnp.einsum(
        "crbt,rcn->btn", series_in, inverse_table(nchan), preferred_element_type=jnp.float32
    )
    return (visibilities, beam_series)


def solution(mesh):
    return jax.shard_map(
        local,
        mesh=mesh,
        in_specs=(P(None, ("groups", "st", "pol"), "br"), P(), P(("st", "pol")), P()),
        out_specs=(
            P(("groups", "br"), ("st", "pol"), None, None),
            P(("groups", "st", "pol"), "br", None),
        ),
        check_vma=False,
    )
```

time: 468 us -> 305 us (0.65)
  other arithmetic: 108 us -> 14.8 us
  matrix products: 78.8 us -> 21.8 us
  Pallas kernels: 0 us -> 46.1 us
  waiting for transfers between devices: 98.8 us -> 68.4 us
  local copies, waits for them, and re-layouts: 58.3 us -> 41.3 us
  between operations: 14.1 us -> 0.79 us
    all_to_all x1, waiting for transfers between devices: 93.1 us -> 0.01 us  [local(): lax.all_to_all(volts, ('st', 'pol'), split_axis=0, concat_axis=0, tiled=T...]
    another operation x3 -> x1, other arithmetic: 80.5 us -> 0.56 us
    ppermute x1 -> x2, waiting for transfers between devices: 5.62 us -> 68.4 us  [the longest x1 62.8 us: local(): lax.ppermute(turned, 'br', [(i, (i + k) % blocks) for i in range(blocks)])]
    dot_general x5 -> x3, matrix products: 78.8 us -> 21.8 us  [the longest x1 10.6 us: local(): jnp.einsum('crbt,rcn->btn', series_in, inverse_table(nchan), preferred_el...]
    pallas_call x0 -> x2, Pallas kernels: none -> 46.1 us  [the longest x1 31.1 us: local(): pl.pallas_call(functools.partial(filter_kernel, ntap), out_shape=jax.Shap...]
    convert_element_type x3, other arithmetic: 25.6 us -> 0.69 us  [the longest x1 0.66 us: local(): station_flags.astype(jnp.float32)[:, None]]
    convert_element_type x2 -> x0, local copies, waits for them, and re-layouts: 20.9 us -> none  [the longest x1 11.2 us: local(): beam_volt = jnp.einsum('corbi,rcit->boct', weights, turned, preferred_ele...]
    mul x0 -> x1, other arithmetic: none -> 6.08 us  [local(): visibilities = jnp.stack([vis_real, vis_imag], axis=2) * time_scale]
  transfers between devices with their start and end apart: 3 -> 3, of which waited for: 2 -> 2; matrix products, arithmetic and copies ran while one was open for 26% -> 19% of each run, Pallas kernels for 0% -> 5%
where the time goes in v1:
time: 305 us; the launch traced here: 304 us
  blocking collectives  98.8 us (32%)
  waiting for transfers between devices  68.4 us (22%)
  Pallas kernels  46.1 us (15%)
  local copies, waits for them, and re-layouts  41.3 us (14%)
  matrix products  21.8 us (7%)
  other arithmetic  14.8 us (5%)
  starting transfers between devices  12.1 us (4%)
    all_to_all x1, blocking collectives, local(): lax.all_to_all(outgoing, ('st', 'pol'), split_axis=0, concat_axis=3, tile...  98.8 us
    ppermute x1, waiting for transfers between devices, local(): lax.ppermute(turned, 'br', [(i, (i + k) % blocks) for i in range(blocks)])  62.8 us
    pallas_call x1, Pallas kernels, local(): pl.pallas_call(functools.partial(filter_kernel, ntap), out_shape=jax.Shap...  31.1 us
    unnamed x13, local copies, waits for them, and re-layouts  30.7 us
    pallas_call x1, Pallas kernels, beams(): pl.pallas_call(functools.partial(beam_kernel, nchan), grid=(per_owner,),...  15 us
    dot_general x1, matrix products, local(): jnp.einsum('crbt,rcn->btn', series_in, inverse_table(nchan), preferred_el...  10.6 us
  transfers between devices with their start and end apart: 3, of which 2 were waited for; matrix products, arithmetic and copies ran while one was open for 19% of the time, Pallas kernels for 5%

profile of v1, /device:TPU:0, one launch (start us, length us, event | category | flops | bytes accessed | tf_op | source)
XLA Modules:
  0.0 304.0 jit_solution(7397109346953253698)
XLA Ops:
  0.6 1.0 slice.21
  1.6 4.9 %collective-permute-start = (bf16[2,64,1408]{2,1,0:T(8,128)(2,1)S(1)}, bf16[2,64,1408]{2,1,0:T(8,128)(2,1)S(1)}, u32[]{:S(2)}, u32[]{:S(2)}) collective-permute-start(bf16[2,64,1408]{2,1,0:T(8,128)(2,1)S(1)} %slice.21), channel_id=1, source_target_pairs={{0,2},{1,3},{4,6},{5,7},{8,10},{9,11},{12,14},{13,15},{16,18},{17,... | collective-permute-start | bytes 1081352 | tf_op jit(solution)/shard_map/ppermute | solution.py:179
  6.5 0.6 negate_select_fusion.4
  7.2 0.7 convert_element_type.38
  7.9 0.7 convert_multiply_fusion.coef
  8.6 5.6 %collective-permute-done.before = bf16[2,64,1408]{2,1,0:T(8,128)(2,1)S(1)} collective-permute-done((bf16[2,64,1408]{2,1,0:T(8,128)(2,1)S(1)}, bf16[2,64,1408]{2,1,0:T(8,128)(2,1)S(1)}, u32[]{:S(2)}, u32[]{:S(2)}) %collective-permute-start) | collective-permute-done | bytes 360480 | tf_op jit(solution)/shard_map/ppermute | solution.py:179
  14.2 0.1 broadcast_in_dim.40.flags
  14.2 0.0 copy-start
  14.2 2.2 copy-done
  16.4 31.1 %shard_map.59 = bf16[256,64,128]{2,1,0:T(8,128)(2,1)S(1)} custom-call(bf16[2,64,16384]{2,1,0:T(8,128)(2,1)S(1)} %copy-done, bf16[2,64,1408]{2,1,0:T(8,128)(2,1)S(1)} %collective-permute-done.before, f32[12,128]{1,0:T(8,128)S(1)} %convert_multiply_fusion.coef, f32[64,128]{1,0:T(8,128)S(1)} %broadcast_in_dim.40.flags, bf16[256,256]{1,0:T(8,128)(2,1)S(1)} %fusion.18.table_hi, ...), custom_call_target="tpu_custom_call" | custom-call | tf_op jit(solution)/shard_map/pallas_call | solution.py:185
  47.5 0.0 copy-start.2
  47.6 98.8 %all_to_all.20 = bf16[8,2,16,64,128]{4,3,2,1,0:T(8,128)(2,1)S(1)} all-to-all(bf16[8,2,16,64,128]{4,3,2,1,0:T(8,128)(2,1)S(1)} %bitcast.29), channel_id=1, replica_groups=mesh['groups'=2,'st'=4,'br'=2,'pol'=2] {'st','pol'}, dimensions={0} | all-to-all | bytes 8388608 | tf_op jit(solution)/shard_map/all_to_all | solution.py:198
  146.4 0.0 copy-start.3
  146.4 3.4 %copy.11 = bf16[1,2,16,8,64,128]{5,4,3,2,1,0:T(8,128)(2,1)} copy(bf16[1,2,16,8,64,128]{5,4,2,1,3,0:T(8,128)(2,1)S(1)} %bitcast.30) | data formatting | bytes 8388608 | tf_op jit(solution)/shard_map/all_to_all | solution.py:198
  149.8 0.0 copy-done.3
  149.8 2.5 collective-permute-start.1
  152.3 0.0 copy-done.2
  152.3 15.0 %shard_map.60 = bf16[8,16,2,64,128]{4,3,2,1,0:T(8,128)(2,1)S(1)} custom-call(s32[512,512]{1,0:T(8,128)S(1)} %copy-done.2, bf16[2,16,512,128]{3,2,1,0:T(8,128)(2,1)} %bitcast.6.x), custom_call_target="tpu_custom_call" | custom-call | flops 4294967296 | bytes 8388608 | tf_op jit(solution)/shard_map/pallas_call | solution.py:153
  167.2 0.0 copy-start.1
  167.2 2.0 copy-done.1
  169.2 4.7 %all-to-all-start.1 = ((bf16[8,16,2,64,128]{4,3,2,1,0:T(8,128)(2,1)}), bf16[8,16,2,64,128]{4,3,2,1,0:T(8,128)(2,1)}, u32[]{:S(2)}, u32[]{:S(2)}) async-start(bf16[8,16,2,64,128]{4,3,2,1,0:T(8,128)(2,1)} %copy-done.1), calls=%async_computation.1 | async-start | bytes 8388608 | tf_op jit(solution)/shard_map/all_to_all | solution.py:202
  173.9 0.6 select_convert_fusion.1
  174.5 3.2 %fusion.48 = (bf16[1,1,16,8,64,128]{5,4,2,1,3,0:T(8,128)(2,1)S(1)}, bf16[1,1,16,8,64,128]{5,4,2,1,3,0:T(8,128)(2,1)S(1)}) fusion(bf16[1,2,16,8,64,128]{5,4,2,1,3,0:T(8,128)(2,1)} %bitcast.31), kind=kLoop, calls=%fused_computation.81 | loop fusion | bytes 8388608 | tf_op jit(solution)/shard_map/slice | solution.py:207
  177.7 0.2 copy.9
  177.9 0.2 copy.10
  178.0 1.9 neg.20
  180.0 62.8 %collective-permute-done.1 = bf16[2,16,512,128]{3,2,1,0:T(8,128)(2,1)} collective-permute-done((bf16[2,16,512,128]{3,2,1,0:T(8,128)(2,1)}, bf16[2,16,512,128]{3,2,1,0:T(8,128)(2,1)}, u32[]{:S(2)}, u32[]{:S(2)}) %collective-permute-start.1) | collective-permute-done | bytes 4194336 | tf_op jit(solution)/shard_map/ppermute | solution.py:206
  242.8 3.2 %fusion.47 = bf16[16,512,128]{2,1,0:T(8,128)(2,1)} fusion(bf16[2,16,512,128]{3,2,1,0:T(8,128)(2,1)} %collective-permute-done.1), kind=kLoop, calls=%fused_computation.80 | loop fusion | flops 1048576 | bytes 4194304 | tf_op jit(solution)/shard_map/neg | solution.py:208
  246.0 2.6 slice_bitcast_fusion.1
  248.5 0.0 copy-start.5
  248.6 1.3 copy-done.5
  249.9 1.0 pad_maximum_fusion
  250.9 5.8 %fusion.9 = f32[256,16,1,512]{0,3,1,2:T(8,128)} fusion(bf16[16,512,512]{2,1,0:T(8,128)(2,1)S(1)} %pad_maximum_fusion, s32[]{:T(128)S(6)} %select_n.128), kind=kOutput, calls=%fused_computation.14 | convolution fusion | flops 2147483648 | bytes 20971524 | tf_op jit(solution)/shard_map/cik,cjk->icj/dot_general | solution.py:214
  256.7 0.0 copy-start.4
  256.7 5.3 %fusion.15 = f32[256,16,1,512]{0,3,1,2:T(8,128)S(1)} fusion(s32[]{:T(128)S(6)} %select_n.128, bf16[16,512,128]{2,1,0:T(8,128)(2,1)S(1)} %bitcast.36, bf16[16,512,128]{2,1,0:T(8,128)(2,1)} %neg.20, bf16[16,512,128]{2,1,0:T(8,128)(2,1)} %copy-done.5, bf16[16,512,128]{2,1,0:T(8,128)(2,1)} %fusion.47, bf16[16,512,128]{2,1,0:T(8,128)(2,1)S(1)} %get-tuple-element.6, ...), kind=kOutput, calls=%fused_computation.16 | convolution fusion | flops 2197815296 | bytes 25165828 | tf_op jit(solution)/shard_map/cik,cjk->icj/dot_general | solution.py:215
  262.0 0.0 copy-done.4
  262.0 6.1 %maximum_multiply_fusion = f32[256,16,2,512]{0,3,1,2:T(8,128)} fusion(f32[256,16,1,512]{0,3,1,2:T(8,128)S(1)} %fusion.15, f32[256,16,1,512]{0,3,1,2:T(8,128)S(1)} %copy-done.4), kind=kLoop, calls=%fused_computation | loop fusion | flops 8388608 | bytes 33554432 | tf_op jit(solution)/shard_map/mul | solution.py:216
  268.1 25.3 %copy.13 = f32[256,16,2,512]{3,2,1,0:T(2,128)} copy(f32[256,16,2,512]{0,3,1,2:T(8,128)} %maximum_multiply_fusion) | data formatting | bytes 33554432
  293.4 0.0 all-to-all-done.1
  293.4 10.6 %fusion.12 = f32[64,128,256]{2,1,0:T(8,128)} fusion(bf16[128,2,64,128]{3,2,1,0:T(8,128)(2,1)} %bitcast.13, bf16[1,128,256]{2,1,0:T(8,128)(2,1)S(1)} %get-tuple-element.11, bf16[1,128,256]{2,1,0:T(8,128)(2,1)S(1)} %get-tuple-element.10), kind=kOutput, calls=%fused_computation.15 | convolution fusion | flops 1073807360 | bytes 12713984 | tf_op jit(solution)/shard_map/crbt,rcn->btn/dot_general | solution.py:219
  (4 shorter events, 0.0 us)
Async XLA Ops:
  1.6 12.5 %collective-permute-start = (bf16[2,64,1408]{2,1,0:T(8,128)(2,1)S(1)}, bf16[2,64,1408]{2,1,0:T(8,128)(2,1)S(1)}, u32[]{:S(2)}, u32[]{:S(2)}) collective-permute-start(bf16[2,64,1408]{2,1,0:T(8,128)(2,1)S(1)} %slice.21), channel_id=1, source_target_pairs={{0,2},{1,3},{4,6},{5,7},{8,10},{9,11},{12,14},{13,15},{16,18},{17,... | collective-permute-start | bytes 1081352 | tf_op jit(solution)/shard_map/ppermute | solution.py:179
  14.2 2.2 copy-start
  47.5 104.7 %copy-start.2 = (s32[512,512]{1,0:T(8,128)S(1)}, s32[512,512]{1,0:T(8,128)}, u32[]{:S(2)}) copy-start(s32[512,512]{1,0:T(8,128)} %delays.1) | copy-start | bytes 3145732
  146.4 3.4 %copy-start.3 = (bf16[8,2,16,64,128]{4,3,2,1,0:T(8,128)(2,1)}, bf16[8,2,16,64,128]{4,3,2,1,0:T(8,128)(2,1)S(1)}, u32[]{:S(2)}) copy-start(bf16[8,2,16,64,128]{4,3,2,1,0:T(8,128)(2,1)S(1)} %all_to_all.20) | copy-start | bytes 12582916
  149.8 93.0 %collective-permute-start.1 = (bf16[2,16,512,128]{3,2,1,0:T(8,128)(2,1)}, bf16[2,16,512,128]{3,2,1,0:T(8,128)(2,1)}, u32[]{:S(2)}, u32[]{:S(2)}) collective-permute-start(bf16[2,16,512,128]{3,2,1,0:T(8,128)(2,1)} %bitcast.6.x), channel_id=1, source_target_pairs={{0,2},{2,0},{1,3},{3,1},{4,6},{6,4},{5,7},{7,5},{8,10},{10,8},{9,1... | collective-permute-start | bytes 12582920 | tf_op jit(solution)/shard_map/ppermute | solution.py:206
  167.2 2.0 copy-start.1
  169.2 124.2 %all-to-all-start.1 = ((bf16[8,16,2,64,128]{4,3,2,1,0:T(8,128)(2,1)}), bf16[8,16,2,64,128]{4,3,2,1,0:T(8,128)(2,1)}, u32[]{:S(2)}, u32[]{:S(2)}) async-start(bf16[8,16,2,64,128]{4,3,2,1,0:T(8,128)(2,1)} %copy-done.1), calls=%async_computation.1 | async-start | bytes 8388608 | tf_op jit(solution)/shard_map/all_to_all | solution.py:202
  248.5 1.3 copy-start.5
  256.7 5.4 %copy-start.4 = (f32[256,16,1,512]{0,3,1,2:T(8,128)S(1)}, f32[256,16,1,512]{0,3,1,2:T(8,128)}, u32[]{:S(2)}) copy-start(f32[256,16,1,512]{0,3,1,2:T(8,128)} %fusion.9) | copy-start | bytes 25165828

commit v2 on v1

--- a/solution.py
+++ b/solution.py
@@ -12,6 +12,7 @@
 LANES = 128
 GROUP = 16
 VMEM = pltpu.VMEM
+MESH = pl.DeviceIdType.MESH
 
 
 def forward_table(nchan, per_owner):
@@ -52,7 +53,8 @@
     block = 8
     for r in range(2):
         for t in range(hist):
-            ext[t] = before[r, rows, t * LANES : (t + 1) * LANES].astype(jnp.float32)
+            past = before[r, rows, t * LANES : (t + 1) * LANES].astype(jnp.float32)
+            ext[t] = jnp.where(lax.axis_index("br") > 0, past, 0.0)
 
         @pl.loop(0, nspec // block)
         def _(tb):
@@ -88,18 +90,124 @@
         turn[pl.ds(s, out.shape[0], stride=GROUP), :] = out
 
 
-def filter_kernel(ntap, samples, before, coef, flags, table_hi, table_lo, out, ext, filt, turn):
-    nrow = out.shape[0]
-
-    @pl.loop(0, samples.shape[1] // GROUP)
+def turn_kernel(
+    ntap, samples, coef, flags, table_hi, table_lo, turned, others,
+    before, send, ext, filt, turn,
+    halo_send, halo_recv, turn_send, turn_recv, share_send, share_recv,
+):
+    nrow, inputs_here = send.shape[0], send.shape[1]
+    groups = inputs_here // GROUP
+    npol = lax.axis_size("pol")
+    owners = lax.axis_size("st") * npol
+    blocks = lax.axis_size("br")
+    me = lax.axis_index("st") * npol + lax.axis_index("pol")
+    slot = lax.axis_index("br")
+    own_rows = nrow // owners
+    tail = before.shape[2]
+    begin = samples.shape[2] - tail
+
+    def owner_id(o):
+        return {"st": o // npol, "pol": lax.rem(o, npol)}
+
+    def block_id(step):
+        return {"br": lax.rem(slot + step, blocks)}
+
+    barrier = pltpu.get_barrier_semaphore()
+    for k in range(1, owners):
+        pl.semaphore_signal(barrier, inc=1, device_id=owner_id(lax.rem(me + k, owners)), device_id_type=MESH)
+    for k in range(1, blocks):
+        pl.semaphore_signal(barrier, inc=1, device_id=block_id(k), device_id_type=MESH)
+    pl.semaphore_wait(barrier, owners + blocks - 2)
+
+    def rows_of(g):
+        return pl.ds(pl.multiple_of(g * GROUP, GROUP), GROUP)
+
+    def place(owner, g):
+        return pl.ds(pl.multiple_of(owner * inputs_here + g * GROUP, GROUP), GROUP)
+
+    def halo(g):
+        return pltpu.make_async_remote_copy(
+            src_ref=samples.at[:, rows_of(g), pl.ds(begin, tail)],
+            dst_ref=before.at[:, rows_of(g), :],
+            send_sem=halo_send.at[g],
+            recv_sem=halo_recv.at[g],
+            device_id=block_id(1),
+            device_id_type=MESH,
+        )
+
+    def corner(g, k):
+        target = lax.rem(me + k, owners)
+        return pltpu.make_async_remote_copy(
+            src_ref=send.at[pl.ds(target * own_rows, own_rows), rows_of(g), :],
+            dst_ref=turned.at[:, place(me, g), :],
+            send_sem=turn_send.at[g, k],
+            recv_sem=turn_recv.at[g, k],
+            device_id=owner_id(target),
+            device_id_type=MESH,
+        )
+
+    def share(g, k, step):
+        at = place(lax.rem(me + owners - k, owners), g)
+        return pltpu.make_async_remote_copy(
+            src_ref=turned.at[:, at, :],
+            dst_ref=others.at[step - 1, :, at, :],
+            send_sem=share_send.at[g, k, step - 1],
+            recv_sem=share_recv.at[g, k, step - 1],
+            device_id=block_id(step),
+            device_id_type=MESH,
+        )
+
+    @pl.loop(0, groups)
     def _(g):
+        halo(g).start()
+
+    def drain(g):
+        @pl.loop(1, owners)
+        def _(k):
+            corner(g, k).wait_recv()
+            for step in range(1, blocks):
+                share(g, k, step).start()
+
+    @pl.loop(0, groups)
+    def _(g):
+        halo(g).wait_recv()
         filter_group(ntap, g, samples, before, coef, flags, table_hi, table_lo, ext, filt, turn)
-        rows = pl.ds(pl.multiple_of(g * GROUP, GROUP), GROUP)
-
-        @pl.loop(0, nrow // 16)
+
+        @pl.loop(0, nrow // own_rows)
         def _(o):
-            part = turn[pl.ds(pl.multiple_of(o * 16 * GROUP, 16 * GROUP), 16 * GROUP), :]
-            out[pl.ds(o * 16, 16), rows, :] = part.reshape(16, GROUP, LANES).astype(jnp.bfloat16)
+            size = own_rows * GROUP
+            part = turn[pl.ds(pl.multiple_of(o * size, size), size), :]
+            send[pl.ds(o * own_rows, own_rows), rows_of(g), :] = part.reshape(
+                own_rows, GROUP, LANES
+            ).astype(jnp.bfloat16)
+
+        @pl.loop(1, owners)
+        def _(k):
+            corner(g, k).start()
+
+        turned[:, place(me, g), :] = send[pl.ds(me * own_rows, own_rows), rows_of(g), :]
+        for step in range(1, blocks):
+            share(g, 0, step).start()
+
+        @pl.when(g >= 2)
+        def _():
+            drain(g - 2)
+
+    for g in range(max(groups - 2, 0), groups):
+        drain(g)
+
+    @pl.loop(0, groups)
+    def _(g):
+        halo(g).wait_send()
+
+        @pl.loop(1, owners)
+        def _(k):
+            corner(g, k).wait_send()
+
+        @pl.loop(0, owners)
+        def _(k):
+            for step in range(1, blocks):
+                share(g, k, step).wait()
 
 
 def cosine(phase, nchan):
@@ -174,36 +282,45 @@
     owners = lax.axis_size("st") * lax.axis_size("pol")
     blocks = lax.axis_size("br")
     per_owner = nchan // owners
-    tail_len = (ntap - 1) * nchan
-    tail = samples[:, :, sample_count - tail_len :]
-    before = lax.ppermute(tail, "br", [(i, i + 1) for i in range(blocks - 1)])
     coefficients = tap_table.astype(jnp.float32) / tap_scale
     flags = jnp.broadcast_to(station_flags.astype(jnp.float32)[:, None], (inputs_here, LANES))
     table = forward_table(nchan, per_owner)
     table_hi = table.astype(jnp.bfloat16)
     table_lo = (table - table_hi.astype(jnp.float32)).astype(jnp.bfloat16)
-    spectra = pl.pallas_call(
-        functools.partial(filter_kernel, ntap),
-        out_shape=jax.ShapeDtypeStruct((2 * nchan, inputs_here, spectra_dev), jnp.bfloat16),
+    groups = inputs_here // GROUP
+    dma = pltpu.SemaphoreType.DMA
+    turned, others = pl.pallas_call(
+        functools.partial(turn_kernel, ntap),
+        out_shape=(
+            jax.ShapeDtypeStruct((2 * per_owner, nin, spectra_dev), jnp.bfloat16),
+            jax.ShapeDtypeStruct((blocks - 1, 2 * per_owner, nin, spectra_dev), jnp.bfloat16),
+        ),
         scratch_shapes=[
+            pltpu.VMEM((2, inputs_here, (ntap - 1) * nchan), jnp.bfloat16),
+            pltpu.VMEM((2 * nchan, inputs_here, spectra_dev), jnp.bfloat16),
             pltpu.VMEM((spectra_dev + ntap - 1, GROUP, LANES), jnp.float32),
             pltpu.VMEM((2, GROUP * spectra_dev, LANES), jnp.float32),
             pltpu.VMEM((2 * nchan * GROUP, LANES), jnp.float32),
+            dma((groups,)),
+            dma((groups,)),
+            dma((groups, owners)),
+            dma((groups, owners)),
+            dma((groups, owners, blocks - 1)),
+            dma((groups, owners, blocks - 1)),
         ],
-        in_specs=[pl.BlockSpec(memory_space=VMEM)] * 6,
-        out_specs=pl.BlockSpec(memory_space=VMEM),
-        compiler_params=pltpu.CompilerParams(vmem_limit_bytes=40 * 2**20),
-    )(samples, before, coefficients, flags, table_hi, table_lo)
-    outgoing = spectra.reshape(owners, 2, per_owner, inputs_here, spectra_dev)
-    arrived = lax.all_to_all(outgoing, ("st", "pol"), split_axis=0, concat_axis=3, tiled=True)
-    turned = arrived.reshape(2, per_owner, nin, spectra_dev)
+        in_specs=[pl.BlockSpec(memory_space=VMEM)] * 5,
+        out_specs=(pl.BlockSpec(memory_space=VMEM), pl.BlockSpec(memory_space=VMEM)),
+        compiler_params=pltpu.CompilerParams(
+            vmem_limit_bytes=40 * 2**20, collective_id=0, has_side_effects=True
+        ),
+    )(samples, coefficients, flags, table_hi, table_lo)
+    turned = turned.reshape(2, per_owner, nin, spectra_dev)
+    others = others.reshape(blocks - 1, 2, per_owner, nin, spectra_dev)
 
     volts = beams(beam_delays, turned, owners, nchan)
     series_in = lax.all_to_all(volts, ("st", "pol"), split_axis=0, concat_axis=0, tiled=True)
 
-    parts = [turned]
-    for k in range(1, blocks):
-        parts.append(lax.ppermute(turned, "br", [(i, (i + k) % blocks) for i in range(blocks)]))
+    parts = [turned] + [others[k] for k in range(blocks - 1)]
     right = jnp.concatenate([p[r] for p in parts for r in (0, 1)], axis=2)
     left_imag = jnp.concatenate([q for p in parts for q in (p[1], -p[0])], axis=2)
     rows_here = nin // blocks

time: 305 us -> 262 us (0.86)
  blocking collectives: 98.8 us -> 0 us
  Pallas kernels: 46.1 us -> 134 us
  waiting for transfers between devices: 68.4 us -> 42.1 us
  local copies, waits for them, and re-layouts: 41.3 us -> 37.3 us
    all_to_all x1 -> x0, blocking collectives: 98.8 us -> none  [local(): lax.all_to_all(outgoing, ('st', 'pol'), split_axis=0, concat_axis=3, tile...]
    pallas_call x1, Pallas kernels: 31.1 us -> 123 us  [local(): pl.pallas_call(functools.partial(turn_kernel, ntap), out_shape=(jax.Shape...]
    ppermute x2 -> x0, waiting for transfers between devices: 68.4 us -> none  [the longest x1 62.8 us: local(): lax.ppermute(turned, 'br', [(i, (i + k) % blocks) for i in range(blocks)])]
    all_to_all x1, waiting for transfers between devices: 0.01 us -> 42.1 us  [local(): lax.all_to_all(volts, ('st', 'pol'), split_axis=0, concat_axis=0, tiled=T...]
    ppermute x2 -> x0, starting transfers between devices: 7.35 us -> none  [the longest x1 4.86 us: local(): before = lax.ppermute(tail, 'br', [(i, i + 1) for i in range(blocks - 1)])]
    all_to_all x1, starting transfers between devices: 4.72 us -> 10.7 us  [local(): lax.all_to_all(volts, ('st', 'pol'), split_axis=0, concat_axis=0, tiled=T...]
    slice x4 -> x0, local copies, waits for them, and re-layouts: 4.55 us -> none  [the longest x3 3.53 us: local(): right = jnp.concatenate([p[r] for p in parts for r in (0, 1)], axis=2)]
    pallas_call x1, Pallas kernels: 15 us -> 10.8 us  [beams(): pl.pallas_call(functools.partial(beam_kernel, nchan), grid=(per_owner,),...]
  transfers between devices with their start and end apart: 3 -> 1, of which waited for: 2 -> 1; matrix products, arithmetic and copies ran while one was open for 19% -> 20% of each run, Pallas kernels for 5% -> 0%
where the time goes in v2:
time: 262 us; the launch traced here: 261 us
  Pallas kernels  134 us (51%)
  waiting for transfers between devices  42.1 us (16%)
  local copies, waits for them, and re-layouts  37.3 us (14%)
  matrix products  21.7 us (8%)
  other arithmetic  15 us (6%)
  starting transfers between devices  10.7 us (4%)
    pallas_call x1, Pallas kernels, local(): pl.pallas_call(functools.partial(turn_kernel, ntap), out_shape=(jax.Shape...  123 us
    all_to_all x1, waiting for transfers between devices, local(): lax.all_to_all(volts, ('st', 'pol'), split_axis=0, concat_axis=0, tiled=T...  42.1 us
    unnamed x17, local copies, waits for them, and re-layouts  34.7 us
    pallas_call x1, Pallas kernels, beams(): pl.pallas_call(functools.partial(beam_kernel, nchan), grid=(per_owner,),...  10.8 us
    all_to_all x1, starting transfers between devices, local(): lax.all_to_all(volts, ('st', 'pol'), split_axis=0, concat_axis=0, tiled=T...  10.7 us
    dot_general x1, matrix products, local(): jnp.einsum('crbt,rcn->btn', series_in, inverse_table(nchan), preferred_el...  10.6 us
    mul x1, other arithmetic, local(): visibilities = jnp.stack([vis_real, vis_imag], axis=2) * time_scale  6.09 us
    dot_general x1, matrix products, local(): jnp.einsum('cik,cjk->icj', left, right, preferred_element_type=jnp.float32)  5.78 us
  transfers between devices with their start and end apart: 1, of which 1 were waited for; matrix products, arithmetic and copies ran while one was open for 20% of the time, Pallas kernels for 0%

profile of v2, /device:TPU:0, one launch (start us, length us, event | category | flops | bytes accessed | tf_op | source)
XLA Modules:
  0.0 261.5 jit_solution(4743803179807747553)
XLA Ops:
  0.7 0.6 negate_select_fusion.4
  1.3 0.7 convert_element_type.38
  2.0 0.7 convert_multiply_fusion.coef
  2.7 0.1 broadcast_in_dim.40.flags
  2.8 0.0 copy-start.1
  2.8 2.2 copy-done.1
  4.9 123.0 %shard_map.59 = (bf16[32,512,128]{2,1,0:T(8,128)(2,1)S(1)}, bf16[1,32,512,128]{3,2,1,0:T(8,128)(2,1)S(1)}) custom-call(bf16[2,64,16384]{2,1,0:T(8,128)(2,1)S(1)} %copy-done.1, f32[12,128]{1,0:T(8,128)S(1)} %convert_multiply_fusion.coef, f32[64,128]{1,0:T(8,128)S(1)} %broadcast_in_dim.40.flags, bf16[256,256]{1,0:T(8,128)(2,1)S(1)} %fusion.18.table_hi, ...), custom_call_target="tpu_custom_call" | custom-call | tf_op jit(solution)/shard_map/pallas_call | solution.py:292
  128.0 0.0 copy-start
  128.0 2.0 copy-done
  130.0 0.0 copy-start.5
  130.0 1.2 copy-done.5
  131.2 10.8 %shard_map.60 = bf16[8,16,2,64,128]{4,3,2,1,0:T(8,128)(2,1)S(1)} custom-call(s32[512,512]{1,0:T(8,128)S(1)} %copy-done.5, bf16[2,16,512,128]{3,2,1,0:T(8,128)(2,1)S(1)} %bitcast.23), custom_call_target="tpu_custom_call" | custom-call | flops 4294967296 | bytes 8388608 | tf_op jit(solution)/shard_map/pallas_call | solution.py:261
  142.0 0.0 copy-start.2
  142.1 2.0 copy-done.2
  144.0 0.0 copy-start.3
  144.0 2.0 copy-done.3
  146.0 10.7 %all-to-all-start = ((bf16[8,16,2,64,128]{4,3,2,1,0:T(8,128)(2,1)}), bf16[8,16,2,64,128]{4,3,2,1,0:T(8,128)(2,1)}, u32[]{:S(2)}, u32[]{:S(2)}) async-start(bf16[8,16,2,64,128]{4,3,2,1,0:T(8,128)(2,1)} %copy-done.2), calls=%async_computation | async-start | bytes 8388608 | tf_op jit(solution)/shard_map/all_to_all | solution.py:321
  156.8 0.0 copy-start.4
  156.8 3.3 %fusion.47 = bf16[16,512,128]{2,1,0:T(8,128)(2,1)} fusion(bf16[1,32,512,128]{3,2,1,0:T(8,128)(2,1)} %copy-done), kind=kLoop, calls=%fused_computation.80 | loop fusion | flops 1048576 | bytes 4194304 | tf_op jit(solution)/shard_map/neg | solution.py:325
  160.1 2.5 slice_bitcast_fusion.1
  162.7 0.0 copy-done.4
  162.7 0.0 copy-start.7
  162.7 2.0 fusion.48
  164.7 0.0 copy-done.7
  164.7 1.0 pad_maximum_fusion
  165.7 5.8 %fusion.9 = f32[256,16,1,512]{0,3,1,2:T(8,128)} fusion(bf16[16,512,512]{2,1,0:T(8,128)(2,1)S(1)} %pad_maximum_fusion, s32[]{:T(128)S(6)} %select_n.128), kind=kOutput, calls=%fused_computation.14 | convolution fusion | flops 2147483648 | bytes 20971524 | tf_op jit(solution)/shard_map/cik,cjk->icj/dot_general | solution.py:331
  171.5 0.0 copy-start.6
  171.5 5.3 %fusion.15 = f32[256,16,1,512]{0,3,1,2:T(8,128)S(1)} fusion(s32[]{:T(128)S(6)} %select_n.128, bf16[16,512,128]{2,1,0:T(8,128)(2,1)S(1)} %get-tuple-element.10, bf16[16,512,128]{2,1,0:T(8,128)(2,1)} %get-tuple-element.9, bf16[16,512,128]{2,1,0:T(8,128)(2,1)} %copy-done.7, bf16[16,512,128]{2,1,0:T(8,128)(2,1)} %fusion.47, ...), kind=kOutput, calls=%fused_computation.16 | convolution fusion | flops 2197815296 | bytes 25165828 | tf_op jit(solution)/shard_map/cik,cjk->icj/dot_general | solution.py:332
  176.9 0.0 copy-done.6
  176.9 6.1 %maximum_multiply_fusion = f32[256,16,2,512]{0,3,1,2:T(8,128)} fusion(f32[256,16,1,512]{0,3,1,2:T(8,128)S(1)} %fusion.15, f32[256,16,1,512]{0,3,1,2:T(8,128)S(1)} %copy-done.6), kind=kLoop, calls=%fused_computation | loop fusion | flops 8388608 | bytes 33554432 | tf_op jit(solution)/shard_map/mul | solution.py:333
  183.0 25.3 %copy.7 = f32[256,16,2,512]{3,2,1,0:T(2,128)} copy(f32[256,16,2,512]{0,3,1,2:T(8,128)} %maximum_multiply_fusion) | data formatting | bytes 33554432
  208.2 0.6 select_convert_fusion.1
  208.8 42.1 %all-to-all-done = bf16[8,16,2,64,128]{4,3,2,1,0:T(8,128)(2,1)} async-done(((bf16[8,16,2,64,128]{4,3,2,1,0:T(8,128)(2,1)}), bf16[8,16,2,64,128]{4,3,2,1,0:T(8,128)(2,1)}, u32[]{:S(2)}, u32[]{:S(2)}) %all-to-all-start) | async-done | bytes 4194336 | tf_op jit(solution)/shard_map/all_to_all | solution.py:321
  250.9 10.6 %fusion.12 = f32[64,128,256]{2,1,0:T(8,128)} fusion(bf16[128,2,64,128]{3,2,1,0:T(8,128)(2,1)} %bitcast.7, bf16[1,128,256]{2,1,0:T(8,128)(2,1)S(1)} %get-tuple-element.14, bf16[1,128,256]{2,1,0:T(8,128)(2,1)S(1)} %get-tuple-element.13), kind=kOutput, calls=%fused_computation.15 | convolution fusion | flops 1073807360 | bytes 12713984 | tf_op jit(solution)/shard_map/crbt,rcn->btn/dot_general | solution.py:336
  (4 shorter events, 0.0 us)
Async XLA Ops:
  2.8 2.2 copy-start.1
  128.0 2.0 copy-start
  130.0 1.2 copy-start.5
  142.0 2.0 copy-start.2
  144.0 2.0 copy-start.3
  146.0 104.8 %all-to-all-start = ((bf16[8,16,2,64,128]{4,3,2,1,0:T(8,128)(2,1)}), bf16[8,16,2,64,128]{4,3,2,1,0:T(8,128)(2,1)}, u32[]{:S(2)}, u32[]{:S(2)}) async-start(bf16[8,16,2,64,128]{4,3,2,1,0:T(8,128)(2,1)} %copy-done.2), calls=%async_computation | async-start | bytes 8388608 | tf_op jit(solution)/shard_map/all_to_all | solution.py:321
  156.8 5.9 %copy-start.4 = (bf16[32,512,128]{2,1,0:T(8,128)(2,1)S(1)}, bf16[32,512,128]{2,1,0:T(8,128)(2,1)}, u32[]{:S(2)}) copy-start(bf16[32,512,128]{2,1,0:T(8,128)(2,1)} %copy-done.3) | copy-start | bytes 12582916
  162.7 2.0 copy-start.7
  171.5 5.4 %copy-start.6 = (f32[256,16,1,512]{0,3,1,2:T(8,128)S(1)}, f32[256,16,1,512]{0,3,1,2:T(8,128)}, u32[]{:S(2)}) copy-start(f32[256,16,1,512]{0,3,1,2:T(8,128)} %fusion.9) | copy-start | bytes 25165828

commit v3 on v2

--- a/solution.py
+++ b/solution.py
@@ -91,8 +91,8 @@
 
 
 def turn_kernel(
-    ntap, samples, coef, flags, table_hi, table_lo, turned, others,
-    before, send, ext, filt, turn,
+    ntap, samples, coef, flags, table_hi, table_lo, delays, turned, others, volts,
+    before, send, ext, filt, turn, weights, w_re, w_im, s_re, s_im,
     halo_send, halo_recv, turn_send, turn_recv, share_send, share_recv,
 ):
     nrow, inputs_here = send.shape[0], send.shape[1]
@@ -193,8 +193,12 @@
         def _():
             drain(g - 2)
 
+    make_weights(me, nrow // 2, own_rows // 2, delays, weights, w_re, w_im, s_re, s_im)
+
     for g in range(max(groups - 2, 0), groups):
         drain(g)
+
+    form_beams(turned, weights, volts)
 
     @pl.loop(0, groups)
     def _(g):
@@ -219,58 +223,41 @@
     return total * z
 
 
-def beam_kernel(nchan, delays, x, out, w_re, w_im, s_re, s_im):
-    c = pl.program_id(0)
-    per_owner = pl.num_programs(0)
-    nbeam, nin = delays.shape
+def make_weights(owner, nchan, per_owner, delays, weights, w_re, w_im, s_re, s_im):
+    nin = delays.shape[1]
     mask = nchan - 1
-
-    @pl.when(c == 0)
-    def _():
-        owner = lax.axis_index("st") * lax.axis_size("pol") + lax.axis_index("pol")
-        d = delays[...]
-        norm = 1.0 / math.sqrt(nin)
-        step = d & mask
-        s_re[...] = cosine(step, nchan)
-        s_im[...] = -cosine((step - nchan // 4) & mask, nchan)
-        first = (d * (owner * per_owner)) & mask
-        w_re[...] = cosine(first, nchan) * norm
-        w_im[...] = -cosine((first - nchan // 4) & mask, nchan) * norm
-
-    re, im = w_re[...], w_im[...]
-    left = jnp.concatenate([re.astype(jnp.bfloat16), (-im).astype(jnp.bfloat16)], axis=1)
-    x_re, x_im = x[0, 0], x[1, 0]
-    right = jnp.concatenate(
-        [jnp.concatenate([x_re, x_im], axis=1), jnp.concatenate([x_im, -x_re], axis=1)], axis=0
-    )
-    volt = jnp.dot(left, right, preferred_element_type=jnp.float32).astype(jnp.bfloat16)
-    nspec = x_re.shape[1]
-    owners, per_beam = out.shape[0], out.shape[3]
-    for o in range(owners):
-        for r in range(2):
-            out[o, 0, r] = volt[o * per_beam : (o + 1) * per_beam, r * nspec : (r + 1) * nspec]
-    a, b = s_re[...], s_im[...]
-    w_re[...] = re * a - im * b
-    w_im[...] = re * b + im * a
-
-
-def beams(beam_delays, turned, owners, nchan):
-    _, per_owner, nin, nspec = turned.shape
-    nbeam = beam_delays.shape[0]
-    plane = pltpu.VMEM((nbeam, nin), jnp.float32)
-    return pl.pallas_call(
-        functools.partial(beam_kernel, nchan),
-        grid=(per_owner,),
-        out_shape=jax.ShapeDtypeStruct((owners, per_owner, 2, nbeam // owners, nspec), jnp.bfloat16),
-        in_specs=[
-            pl.BlockSpec((nbeam, nin), lambda c: (0, 0)),
-            pl.BlockSpec((2, 1, nin, nspec), lambda c: (0, c, 0, 0)),
-        ],
-        out_specs=pl.BlockSpec((owners, 1, 2, nbeam // owners, nspec), lambda c: (0, c, 0, 0, 0)),
-        scratch_shapes=[plane] * 4,
-        compiler_params=pltpu.CompilerParams(vmem_limit_bytes=40 * 2**20),
-        cost_estimate=pl.CostEstimate(flops=2**32, bytes_accessed=2**23, transcendentals=0),
-    )(beam_delays, turned)
+    norm = 1.0 / math.sqrt(nin)
+    d = delays[...]
+    step = d & mask
+    s_re[...] = cosine(step, nchan)
+    s_im[...] = -cosine((step - nchan // 4) & mask, nchan)
+    first = (d * (owner * per_owner)) & mask
+    w_re[...] = cosine(first, nchan) * norm
+    w_im[...] = -cosine((first - nchan // 4) & mask, nchan) * norm
+
+    @pl.loop(0, per_owner)
+    def _(c):
+        re, im = w_re[...], w_im[...]
+        weights[c, :, :nin] = re.astype(jnp.bfloat16)
+        weights[c, :, nin:] = (-im).astype(jnp.bfloat16)
+        a, b = s_re[...], s_im[...]
+        w_re[...] = re * a - im * b
+        w_im[...] = re * b + im * a
+
+
+def form_beams(turned, weights, volts):
+    owners, per_owner, _, per_beam, nspec = volts.shape
+
+    @pl.loop(0, per_owner)
+    def _(c):
+        x_re, x_im = turned[c], turned[per_owner + c]
+        right = jnp.concatenate(
+            [jnp.concatenate([x_re, x_im], axis=1), jnp.concatenate([x_im, -x_re], axis=1)], axis=0
+        )
+        volt = jnp.dot(weights[c], right, preferred_element_type=jnp.float32).astype(jnp.bfloat16)
+        for o in range(owners):
+            for r in range(2):
+                volts[o, c, r] = volt[o * per_beam : (o + 1) * per_beam, r * nspec : (r + 1) * nspec]
 
 
 def local(samples, tap_table, station_flags, beam_delays):
@@ -289,11 +276,14 @@
     table_lo = (table - table_hi.astype(jnp.float32)).astype(jnp.bfloat16)
     groups = inputs_here // GROUP
     dma = pltpu.SemaphoreType.DMA
-    turned, others = pl.pallas_call(
+    nbeam = beam_delays.shape[0]
+    plane = pltpu.VMEM((nbeam, nin), jnp.float32)
+    turned, others, volts = pl.pallas_call(
         functools.partial(turn_kernel, ntap),
         out_shape=(
             jax.ShapeDtypeStruct((2 * per_owner, nin, spectra_dev), jnp.bfloat16),
             jax.ShapeDtypeStruct((blocks - 1, 2 * per_owner, nin, spectra_dev), jnp.bfloat16),
+            jax.ShapeDtypeStruct((owners, per_owner, 2, nbeam // owners, spectra_dev), jnp.bfloat16),
         ),
         scratch_shapes=[
             pltpu.VMEM((2, inputs_here, (ntap - 1) * nchan), jnp.bfloat16),
@@ -301,6 +291,11 @@
             pltpu.VMEM((spectra_dev + ntap - 1, GROUP, LANES), jnp.float32),
             pltpu.VMEM((2, GROUP * spectra_dev, LANES), jnp.float32),
             pltpu.VMEM((2 * nchan * GROUP, LANES), jnp.float32),
+            pltpu.VMEM((per_owner, nbeam, 2 * nin), jnp.bfloat16),
+            plane,
+            plane,
+            plane,
+            plane,
             dma((groups,)),
             dma((groups,)),
             dma((groups, owners)),
@@ -308,16 +303,15 @@
             dma((groups, owners, blocks - 1)),
             dma((groups, owners, blocks - 1)),
         ],
-        in_specs=[pl.BlockSpec(memory_space=VMEM)] * 5,
-        out_specs=(pl.BlockSpec(memory_space=VMEM), pl.BlockSpec(memory_space=VMEM)),
+        in_specs=[pl.BlockSpec(memory_space=VMEM)] * 6,
+        out_specs=(pl.BlockSpec(memory_space=VMEM),) * 3,
         compiler_params=pltpu.CompilerParams(
-            vmem_limit_bytes=40 * 2**20, collective_id=0, has_side_effects=True
+            vmem_limit_bytes=54 * 2**20, collective_id=0, has_side_effects=True
         ),
-    )(samples, coefficients, flags, table_hi, table_lo)
+    )(samples, coefficients, flags, table_hi, table_lo, beam_delays)
     turned = turned.reshape(2, per_owner, nin, spectra_dev)
     others = others.reshape(blocks - 1, 2, per_owner, nin, spectra_dev)
 
-    volts = beams(beam_delays, turned, owners, nchan)
     series_in = lax.all_to_all(volts, ("st", "pol"), split_axis=0, concat_axis=0, tiled=True)
 
     parts = [turned] + [others[k] for k in range(blocks - 1)]

time: 262 us -> 255 us (0.973)
  local copies, waits for them, and re-layouts: 37.3 us -> 28.5 us
    pallas_call x1 -> x0, Pallas kernels: 10.8 us -> none  [beams(): pl.pallas_call(functools.partial(beam_kernel, nchan), grid=(per_owner,),...]
    unnamed x17 -> x7, local copies, waits for them, and re-layouts: 34.7 us -> 25.3 us
    pallas_call x1, Pallas kernels: 123 us -> 132 us  [local(): pl.pallas_call(functools.partial(turn_kernel, ntap), out_shape=(jax.Shape...]
where the time goes in v3:
time: 255 us; the launch traced here: 254 us
  Pallas kernels  132 us (52%)
  waiting for transfers between devices  42.1 us (17%)
  local copies, waits for them, and re-layouts  28.5 us (11%)
  matrix products  21.8 us (9%)
  other arithmetic  16.9 us (7%)
  starting transfers between devices  12.2 us (5%)
    pallas_call x1, Pallas kernels, local(): pl.pallas_call(functools.partial(turn_kernel, ntap), out_shape=(jax.Shape...  132 us
    all_to_all x1, waiting for transfers between devices, local(): lax.all_to_all(volts, ('st', 'pol'), split_axis=0, concat_axis=0, tiled=T...  42.1 us
    unnamed x7, local copies, waits for them, and re-layouts  25.3 us
    all_to_all x1, starting transfers between devices, local(): lax.all_to_all(volts, ('st', 'pol'), split_axis=0, concat_axis=0, tiled=T...  12.2 us
    dot_general x1, matrix products, local(): jnp.einsum('crbt,rcn->btn', series_in, inverse_table(nchan), preferred_el...  10.6 us
    mul x1, other arithmetic, local(): visibilities = jnp.stack([vis_real, vis_imag], axis=2) * time_scale  6.06 us
    dot_general x1, matrix products, local(): jnp.einsum('cik,cjk->icj', left, right, preferred_element_type=jnp.float32)  5.79 us
    dot_general x1, matrix products, local(): jnp.einsum('cik,cjk->icj', left_imag, right, preferred_element_type=jnp.f...  5.35 us
  transfers between devices with their start and end apart: 1, of which 1 were waited for; matrix products, arithmetic and copies ran while one was open for 20% of the time, Pallas kernels for 0%

profile of v3, /device:TPU:0, one launch (start us, length us, event | category | flops | bytes accessed | tf_op | source)
XLA Modules:
  0.0 254.5 jit_solution(11800812918451539582)
XLA Ops:
  0.7 0.6 negate_select_fusion.4
  1.3 0.7 subtract_convert_fusion.table_lo
  1.9 0.7 fusion.18.table_hi
  2.6 0.7 convert_element_type.38
  3.3 1.3 convert_multiply_fusion.coef
  4.6 0.7 broadcast_in_dim.40.flags
  5.2 132.3 %shard_map.59 = (bf16[32,512,128]{2,1,0:T(8,128)(2,1)}, bf16[1,32,512,128]{3,2,1,0:T(8,128)(2,1)}, bf16[8,16,2,64,128]{4,3,2,1,0:T(8,128)(2,1)}) custom-call(bf16[2,64,16384]{2,1,0:T(8,128)(2,1)} %samples.1, f32[12,128]{1,0:T(8,128)} %convert_multiply_fusion.coef, f32[64,128]{1,0:T(8,128)} %broadcast_in_dim.40.flags, bf16[256,256]{1,0:T(8,128)(2,1)} %fusion.18.table_hi, ...), custom_call_target="tpu_custom_call" | custom-call | tf_op jit(solution)/shard_map/pallas_call | solution.py:281
  137.5 12.2 %all-to-all-start = ((bf16[8,16,2,64,128]{4,3,2,1,0:T(8,128)(2,1)}), bf16[8,16,2,64,128]{4,3,2,1,0:T(8,128)(2,1)}, u32[]{:S(2)}, u32[]{:S(2)}) async-start(bf16[8,16,2,64,128]{4,3,2,1,0:T(8,128)(2,1)} %get-tuple-element.7), calls=%async_computation | async-start | bytes 8388608 | tf_op jit(solution)/shard_map/all_to_all | solution.py:315
  149.7 0.0 copy-start.2
  149.7 3.4 %fusion.47 = bf16[16,512,128]{2,1,0:T(8,128)(2,1)} fusion(bf16[1,32,512,128]{3,2,1,0:T(8,128)(2,1)} %get-tuple-element.6), kind=kLoop, calls=%fused_computation.80 | loop fusion | flops 1048576 | bytes 4194304 | tf_op jit(solution)/shard_map/neg | solution.py:319
  153.1 2.5 slice_bitcast_fusion.1
  155.7 0.0 copy-start.1
  155.7 0.0 copy-done.2
  155.7 2.0 fusion.48
  157.7 0.0 copy-done.1
  157.7 1.0 pad_maximum_fusion
  158.7 5.8 %fusion.9 = f32[256,16,1,512]{0,3,1,2:T(8,128)} fusion(bf16[16,512,512]{2,1,0:T(8,128)(2,1)S(1)} %pad_maximum_fusion, s32[]{:T(128)S(6)} %select_n.128), kind=kOutput, calls=%fused_computation.14 | convolution fusion | flops 2147483648 | bytes 20971524 | tf_op jit(solution)/shard_map/cik,cjk->icj/dot_general | solution.py:325
  164.5 0.0 copy-start
  164.5 5.4 %fusion.15 = f32[256,16,1,512]{0,3,1,2:T(8,128)S(1)} fusion(s32[]{:T(128)S(6)} %select_n.128, bf16[16,512,128]{2,1,0:T(8,128)(2,1)S(1)} %get-tuple-element.12, bf16[16,512,128]{2,1,0:T(8,128)(2,1)} %get-tuple-element.11, bf16[16,512,128]{2,1,0:T(8,128)(2,1)} %copy-done.1, bf16[16,512,128]{2,1,0:T(8,128)(2,1)} %fusion.47, ...), kind=kOutput, calls=%fused_computation.16 | convolution fusion | flops 2197815296 | bytes 25165828 | tf_op jit(solution)/shard_map/cik,cjk->icj/dot_general | solution.py:326
  169.9 0.0 copy-done
  169.9 6.1 %maximum_multiply_fusion = f32[256,16,2,512]{0,3,1,2:T(8,128)} fusion(f32[256,16,1,512]{0,3,1,2:T(8,128)S(1)} %fusion.15, f32[256,16,1,512]{0,3,1,2:T(8,128)S(1)} %copy-done), kind=kLoop, calls=%fused_computation | loop fusion | flops 8388608 | bytes 33554432 | tf_op jit(solution)/shard_map/mul | solution.py:327
  176.0 25.3 %copy.7 = f32[256,16,2,512]{3,2,1,0:T(2,128)} copy(f32[256,16,2,512]{0,3,1,2:T(8,128)} %maximum_multiply_fusion) | data formatting | bytes 33554432
  201.2 0.6 select_convert_fusion.1
  201.8 42.1 %all-to-all-done = bf16[8,16,2,64,128]{4,3,2,1,0:T(8,128)(2,1)} async-done(((bf16[8,16,2,64,128]{4,3,2,1,0:T(8,128)(2,1)}), bf16[8,16,2,64,128]{4,3,2,1,0:T(8,128)(2,1)}, u32[]{:S(2)}, u32[]{:S(2)}) %all-to-all-start) | async-done | bytes 4194336 | tf_op jit(solution)/shard_map/all_to_all | solution.py:315
  243.9 10.6 %fusion.12 = f32[64,128,256]{2,1,0:T(8,128)} fusion(bf16[128,2,64,128]{3,2,1,0:T(8,128)(2,1)} %bitcast.6, bf16[1,128,256]{2,1,0:T(8,128)(2,1)S(1)} %get-tuple-element.16, bf16[1,128,256]{2,1,0:T(8,128)(2,1)S(1)} %get-tuple-element.15), kind=kOutput, calls=%fused_computation.15 | convolution fusion | flops 1073807360 | bytes 12713984 | tf_op jit(solution)/shard_map/crbt,rcn->btn/dot_general | solution.py:330
  (2 shorter events, 0.0 us)
Async XLA Ops:
  137.5 106.4 %all-to-all-start = ((bf16[8,16,2,64,128]{4,3,2,1,0:T(8,128)(2,1)}), bf16[8,16,2,64,128]{4,3,2,1,0:T(8,128)(2,1)}, u32[]{:S(2)}, u32[]{:S(2)}) async-start(bf16[8,16,2,64,128]{4,3,2,1,0:T(8,128)(2,1)} %get-tuple-element.7), calls=%async_computation | async-start | bytes 8388608 | tf_op jit(solution)/shard_map/all_to_all | solution.py:315
  149.7 6.0 %copy-start.2 = (bf16[32,512,128]{2,1,0:T(8,128)(2,1)S(1)}, bf16[32,512,128]{2,1,0:T(8,128)(2,1)}, u32[]{:S(2)}) copy-start(bf16[32,512,128]{2,1,0:T(8,128)(2,1)} %get-tuple-element.5) | copy-start | bytes 12582916
  155.7 2.0 copy-start.1
  164.5 5.4 %copy-start = (f32[256,16,1,512]{0,3,1,2:T(8,128)S(1)}, f32[256,16,1,512]{0,3,1,2:T(8,128)}, u32[]{:S(2)}) copy-start(f32[256,16,1,512]{0,3,1,2:T(8,128)} %fusion.9) | copy-start | bytes 25165828
